TPU v7x, 32 devices: a whole 2x2x4 slice. The times are simulated.
32 devices in a mesh: rad: 4 (over y, core), ang: 8 (over z, x).
Axes of the slice: x: 2, y: 2, z: 4, core: 2. Of those that a mesh axis runs over, the one named last changes fastest.
Arguments:
- source_coeffs: bfloat16 [512, 512, 2, 128], P('ang', 'rad'), may hold values from -6 to 6
- inverses: bfloat16 [512, 128, 128], P('rad')
- velocity: bfloat16 [2, 768, 128, 1536], P(None, 'ang', 'rad'), may hold values from -6 to 6
- order_slots: int32 [512], replicated, may hold values from 0 to 511, as said below
Outputs:
- advected: bfloat16 [512, 2, 128, 512], P('ang', None, 'rad')
Inputs may be any that keep to these rules, and one draw needn't show every extreme that they name: `order_slots`: the slots form 512 // 64 consecutive blocks of 64; in each block the first 32 slots hold distinct orders below 256, and slot 32 + i of a block holds 511 minus the order in slot i of that block; every order appears exactly once.
All inputs are finite; a program needn't handle non-finite values.
Results may differ from a plain program's by a relative error of at most 0.012.
Values may be sent and summed in bfloat16 or wider, within the bound.
A program may use at most 320 MiB of HBM per device.

v0:
```python
import math

import jax
import jax.numpy as jnp
from jax import lax
from jax.sharding import PartitionSpec as P

inner_radius = 0.35
rescale_bound = 1e20
rescale_log = 46.051701859880914
start_log = -1.2051210046670229


def legendre_rows(orders, degree_count, lat_count):
    colatitude = (jnp.arange(lat_count, dtype=jnp.float32) + 0.5) * (math.pi / lat_count)
    cosines = jnp.cos(colatitude)[None, :]
    sines = jnp.sin(colatitude)[None, :]
    order_value = orders.astype(jnp.float32)[:, None]
    orders_col = orders[:, None]
    log_start = (
        start_log
        + 0.5 * (lax.lgamma(order_value + 1.5) - lax.lgamma(order_value + 1.0))
        + order_value * jnp.log(sines)
    )
    zero_field = jnp.zeros((orders.shape[0], lat_count), jnp.float32)

    def advance(state_carry, degree):
        prev_one, prev_two, log_scale = state_carry
        degree_value = degree.astype(jnp.float32)
        denominator = jnp.maximum(degree_value * degree_value - order_value * order_value, 1.0)
        recur_a = jnp.sqrt(jnp.maximum(4.0 * degree_value * degree_value - 1.0, 1.0) / denominator)
        lower_sq = (degree_value - 1.0) * (degree_value - 1.0)
        recur_b = jnp.sqrt(
            jnp.maximum(lower_sq - order_value * order_value, 0.0)
            / jnp.maximum(4.0 * lower_sq - 1.0, 1.0)
        )
        grown_value = recur_a * (cosines * prev_one - recur_b * prev_two)
        before = degree < orders_col
        starting = degree == orders_col
        current = jnp.where(before, 0.0, jnp.where(starting, 1.0, grown_value))
        previous = jnp.where(before | starting, 0.0, prev_one)
        too_large = jnp.abs(current) > rescale_bound
        factor = jnp.where(too_large, 1.0 / rescale_bound, 1.0)
        log_scale = log_scale + jnp.where(too_large, rescale_log, 0.0)
        current = current * factor
        previous = previous * factor
        value_scaled = current * jnp.exp(log_scale)
        return ((current, previous, log_scale), value_scaled.astype(jnp.bfloat16))

    _, legendre = lax.scan(
        advance, (zero_field, zero_field, log_start), jnp.arange(degree_count, dtype=jnp.int32)
    )
    return legendre


def radial_tables(mode_count, radius_count):
    angles = (jnp.arange(radius_count, dtype=jnp.float32) + 0.5) * (math.pi / radius_count)
    mode_values = jnp.arange(mode_count, dtype=jnp.float32)[:, None]
    values = jnp.cos(mode_values * angles[None, :])
    slopes = (
        mode_values
        * jnp.sin(mode_values * angles[None, :])
        / jnp.sin(angles)[None, :]
        * (2.0 / (1.0 - inner_radius))
    )
    return jnp.stack([values, slopes])


def fourier_tables(orders, lon_count):
    phase_index = orders[:, None] * jnp.arange(lon_count, dtype=jnp.int32)[None, :] % lon_count
    phase_angle = phase_index.astype(jnp.float32) * (2.0 * math.pi / lon_count)
    weight = jnp.where(orders == 0, 1.0, 2.0).astype(jnp.float32)[:, None]
    cosine = jnp.cos(phase_angle)
    sine = jnp.sin(phase_angle)
    synth_table = jnp.stack([weight * cosine, -weight * sine], 1).astype(jnp.bfloat16)
    analyse_table = (jnp.stack([cosine, -sine], 1) * (2.0 * math.pi / lon_count)).astype(
        jnp.bfloat16
    )
    return (synth_table, analyse_table)


def azimuthal(lat_values, orders):
    order_value = orders.astype(jnp.float32)[:, None, None]
    real_part = lat_values[:, 0].astype(jnp.float32)
    imag_part = lat_values[:, 1].astype(jnp.float32)
    return jnp.stack([-order_value * imag_part, order_value * real_part], 1).astype(jnp.bfloat16)


def local(source_coeffs, inverses, velocity, order_slots):
    slots_local, degrees_local, _, mode_count = source_coeffs.shape
    lat_local = velocity.shape[1]
    radii_local = velocity.shape[2]
    lon_count = velocity.shape[3]
    rad_count = lax.axis_size("rad")
    ang_count = lax.axis_size("ang")
    degree_count = degrees_local * rad_count
    lat_count = lat_local * ang_count
    radius_count = radii_local * rad_count
    rad_index = lax.axis_index("rad")
    ang_index = lax.axis_index("ang")
    my_orders = lax.dynamic_slice_in_dim(order_slots, ang_index * slots_local, slots_local, 0)
    degrees = rad_index * degrees_local + jnp.arange(degrees_local, dtype=jnp.int32)
    degree_mask = (degrees[None, :] >= my_orders[:, None]).astype(jnp.float32)
    solved = (
        jnp.einsum("lkj,slcj->slck", inverses, source_coeffs, preferred_element_type=jnp.float32)
        * degree_mask[:, :, None, None]
    )
    tables = radial_tables(mode_count, radius_count)
    radial = jnp.einsum("slck,fki->sfcli", solved, tables, precision=lax.Precision.HIGHEST).astype(
        jnp.bfloat16
    )
    radial = lax.all_to_all(radial, "rad", split_axis=4, concat_axis=3, tiled=True)
    legendre = legendre_rows(my_orders, degree_count, lat_count)
    lat_spec = jnp.einsum(
        "sfcli,lsj->sfcij", radial, legendre, preferred_element_type=jnp.float32
    ).astype(jnp.bfloat16)
    received = lax.all_to_all(lat_spec, "ang", split_axis=4, concat_axis=0, tiled=True)
    fields = jnp.concatenate([received, azimuthal(received[:, 0], order_slots)[:, None]], 1)
    synth_table, analyse_table = fourier_tables(order_slots, lon_count)
    physical = jnp.einsum(
        "sfcij,scn->fjin", fields, synth_table, preferred_element_type=jnp.float32
    )
    lat_rows = ang_index * lat_local + jnp.arange(lat_local, dtype=jnp.int32)
    colatitude = (lat_rows.astype(jnp.float32) + 0.5) * (math.pi / lat_count)
    sines = jnp.sin(colatitude)
    quad_weight = math.pi / lat_count * sines
    radius_rows = rad_index * radii_local + jnp.arange(radii_local, dtype=jnp.int32)
    angles = (radius_rows.astype(jnp.float32) + 0.5) * (math.pi / radius_count)
    radius_col = (inner_radius + (1.0 - inner_radius) * (jnp.cos(angles) + 1.0) * 0.5)[
        None, :, None
    ]
    flux_term = velocity[0].astype(jnp.float32) * (
        physical[1] + 3.0 * physical[0] / radius_col
    ) + velocity[1].astype(jnp.float32) * physical[2] / (radius_col * sines[:, None, None])
    flux_term = flux_term.astype(jnp.bfloat16)
    fourier = jnp.einsum(
        "jin,scn->scij", flux_term, analyse_table, preferred_element_type=jnp.float32
    )
    fourier = (fourier * quad_weight[None, None, None, :]).astype(jnp.bfloat16)
    fourier = lax.all_to_all(fourier, "ang", split_axis=0, concat_axis=3, tiled=True)
    advected = jnp.einsum(
        "scij,lsj->scil", fourier, legendre, preferred_element_type=jnp.float32
    ).astype(jnp.bfloat16)
    return advected


def solution(mesh):
    in_specs = (P("ang", "rad", None, None), P("rad", None, None), P(None, "ang", "rad", None), P())
    out_specs = P("ang", None, "rad", None)
    return jax.shard_map(local, mesh=mesh, in_specs=in_specs, out_specs=out_specs, check_vma=False)
```

profile of v0, /device:TPU:0, one launch (start us, length us, event | category | flops | bytes accessed | tf_op | source)
XLA Modules:
  0.0 2484.1 jit_solution(14780317178522321386)
XLA Ops:
  1.2 6.9 bitcast_multiply_fusion
  8.1 21.1 convert_bitcast_fusion
  29.2 18.7 copy.43
  47.9 5.6 all-to-all-start
  53.8 1513.6 %while.20 = (s32[]{:T(128)}, f32[64,768]{1,0:T(8,128)S(1)}, f32[64,768]{1,0:T(8,128)S(1)}, f32[64,768]{1,0:T(8,128)S(1)}, bf16[512,64,768]{2,1,0:T(8,128)(2,1)},...) while((s32[]{:T(128)}, f32[64,768]{1,0:T(8,128)S(1)}, ...), condition=%wide.region_1.2_spmd.clone, body=%wide.region_0.1_spmd.clone.sunk | while | flops 1427534 | bytes 2076968 | solution.py:50
  76.6 0.9 fusion.88
  203.7 0.9 fusion.88
  277.6 0.9 fusion.88
  280.5 0.9 fusion.88
  333.8 0.9 fusion.88
  339.7 0.9 fusion.88
  351.5 0.9 fusion.88
  425.5 0.9 fusion.88
  549.6 0.9 fusion.88
  594.0 0.9 fusion.88
  629.5 0.9 fusion.88
  730.0 0.9 fusion.88
  747.7 0.9 fusion.88
  919.2 0.9 fusion.88
  936.9 0.9 fusion.88
  990.1 0.9 fusion.88
  1031.5 0.9 fusion.88
  1374.4 0.9 fusion.88
  1398.0 0.9 fusion.88
  1445.3 0.9 fusion.88
  1463.0 0.9 fusion.88
  1567.4 12.2 copy.102
  1579.6 13.1 all_to_all.42
  1592.7 58.3 %fusion.31 = bf16[64,2,2,32,768]{4,3,2,1,0:T(8,128)(2,1)} fusion(bf16[64,2,2,512,32]{3,4,2,1,0:T(8,128)(2,1)} %all_to_all.42, bf16[512,64,768,1,1]{2,1,0,4,3:T(8,128)(2,1)} %bitcast.154), kind=kOutput, calls=%fused_computation.49 | convolution fusion | flops 6448742400 | bytes 71303168 | tf_op jit(solution)/shard_map/sfcli,lsj->sfcij/dot_general | solution.py:114
  1651.0 42.9 %copy.46 = bf16[64,2,2,32,768]{0,3,2,1,4:T(8,128)(2,1)} copy(bf16[64,2,2,32,768]{4,3,2,1,0:T(8,128)(2,1)} %fusion.31) | data formatting | bytes 25165824 | tf_op jit(solution)/shard_map/convert_element_type | solution.py:116
  1693.9 22.6 reshape.597
  1716.5 7.4 all-to-all-start.1
  1724.1 15.8 fusion.59
  1739.9 14.4 fusion.82
  1754.3 243.2 %all-to-all-done.1 = bf16[8,2,393216]{2,1,0:T(2,128)(2,1)} async-done(((bf16[8,2,393216]{2,1,0:T(2,128)(2,1)}), bf16[8,2,393216]{2,1,0:T(2,128)(2,1)}, u32[]{:S(2)}, u32[]{:S(2)}) %all-to-all-start.1) | async-done | bytes 12582944 | tf_op jit(solution)/shard_map/all_to_all | solution.py:117
  1997.6 22.5 reshape.598
  2020.0 44.4 %copy.47 = bf16[64,2,2,32,8,96]{5,3,2,1,0,4:T(8,128)(2,1)} copy(bf16[64,2,2,32,8,96]{0,3,2,1,5,4:T(8,128)(2,1)} %bitcast.149) | data formatting | bytes 25165824 | tf_op jit(solution)/shard_map/all_to_all | solution.py:117
  2064.4 8.7 slice.32
  2073.1 25.6 %copy.50 = bf16[512,2,2,32,96]{0,4,2,3,1:T(8,128)(2,1)} copy(bf16[512,2,2,32,96]{4,3,2,1,0:T(8,128)(2,1)} %bitcast.147) | data formatting | bytes 25165824 | tf_op jit(solution)/shard_map/all_to_all | solution.py:117
  2098.7 13.4 copy.67
  2112.1 5.4 fusion.49
  2117.6 38.8 %convolution_bitcast_fusion = f32[3,96,32,1536]{3,1,2,0:T(8,128)} fusion(bf16[512,1,1,32,96]{0,4,2,3,1:T(8,128)(2,1)} %get-tuple-element.209, bf16[512,1,1,32,96]{0,4,2,3,1:T(8,128)(2,1)} %get-tuple-element.208, bf16[512,2,2,32,96]{0,4,2,3,1:T(8,128)(2,1)} %copy.50, bf16[512,1,1536]{2,0,1:T(8,128)(2,1)} %get-tuple-element.212, ...), kind=kOutput, calls=%fused_computation.22 | convolution fusion | flops 29053943808 | bytes 78643200 | tf_op jit(solution)/shard_map/sfcij,scn->fjin/dot_general | solution.py:120
  2156.3 40.4 %fusion.34 = bf16[512,2,32,96]{0,3,2,1:T(8,128)(2,1)} fusion(f32[96]{0:T(128)S(1)} %get-tuple-element.220, f32[96,32]{0,1:T(8,128)S(1)} %broadcast_multiply_fusion, f32[3,96,32,1536]{3,1,2,0:T(8,128)} %convolution_bitcast_fusion, bf16[1,96,32,1536]{3,2,1,0:T(8,128)(2,1)} %get-tuple-element.207, f32[32]{0:T(128)S(1)} %multiply_add_fusion.1, ...), kind=kOutput, calls=%fused_computation.50 | convolution fusion | flops 9721872384 | bytes 88093184 | tf_op jit(solution)/shard_map/jin,scn->scij/dot_general | solution.py:136
  2196.7 14.2 copy.52
  2210.9 189.0 %all_to_all.54 = bf16[512,2,32,96]{3,2,1,0:T(8,128)(2,1)} all-to-all(bf16[512,2,32,96]{3,2,1,0:T(8,128)(2,1)} %copy.52), channel_id=1, replica_groups=mesh['rad'=4,'ang'=8] {'ang'}, dimensions={0} | all-to-all | bytes 12582912 | tf_op jit(solution)/shard_map/all_to_all | solution.py:140
  2399.9 23.1 copy.53
  2423.0 13.8 all_to_all.50
  2436.8 47.0 %fusion.62 = bf16[64,2,32,512]{3,2,1,0:T(8,128)(2,1)} fusion(bf16[64,2,32,768]{3,2,1,0:T(8,128)(2,1)} %all_to_all.50, bf16[512,64,768,1]{2,1,0,3:T(8,128)(2,1)} %bitcast.155), kind=kOutput, calls=%fused_computation.77 | convolution fusion | flops 3223322624 | bytes 60817408 | tf_op jit(solution)/shard_map/scij,lsj->scil/dot_general | solution.py:141
  (3584 shorter events, 1180.0 us)
Async XLA Ops:
  47.9 1519.5 %all-to-all-start = ((bf16[64,2,2,128,128]{3,2,0,1,4:T(2,128)(2,1)}), bf16[64,2,2,128,128]{3,2,0,1,4:T(2,128)(2,1)}, u32[]{:S(2)}, u32[]{:S(2)}) async-start(bf16[64,2,2,128,128]{3,2,0,1,4:T(2,128)(2,1)} %copy.43), calls=%async_computation | async-start | bytes 16777216 | tf_op jit(solution)/shard_map/all_to_all | solution.py:112
  1716.5 7.4 copy-start
  1716.5 281.1 %all-to-all-start.1 = ((bf16[8,2,393216]{2,1,0:T(2,128)(2,1)}), bf16[8,2,393216]{2,1,0:T(2,128)(2,1)}, u32[]{:S(2)}, u32[]{:S(2)}) async-start(bf16[8,2,393216]{2,1,0:T(2,128)(2,1)} %reshape.597), calls=%async_computation.1 | async-start | bytes 25165824 | tf_op jit(solution)/shard_map/all_to_all | solution.py:117
where the time goes:
time: 2500 us; the launch traced here: 2480 us
  other arithmetic  912 us (36%)
  local copies, waits for them, and re-layouts  598 us (24%)
  loops' own time  316 us (13%)
  waiting for transfers between devices  243 us (10%)
  matrix products  212 us (8%)
  blocking collectives  189 us (8%)
    dynamic_update_slice x512, other arithmetic, legendre_rows(): lax.scan(advance, (zero_field, zero_field, log_start), jnp.arange(degree_...  456 us
    another operation x1, loops' own time, legendre_rows(): lax.scan(advance, (zero_field, zero_field, log_start), jnp.arange(degree_...  316 us
    dynamic_slice x512, local copies, waits for them, and re-layouts, legendre_rows(): lax.scan(advance, (zero_field, zero_field, log_start), jnp.arange(degree_...  302 us
    or x512, other arithmetic, advance(): previous = jnp.where(before | starting, 0.0, prev_one)  289 us
    all_to_all x1, waiting for transfers between devices, local(): lax.all_to_all(lat_spec, 'ang', split_axis=4, concat_axis=0, tiled=True)  243 us
    all_to_all x1, blocking collectives, local(): lax.all_to_all(fourier, 'ang', split_axis=0, concat_axis=3, tiled=True)  189 us
    mul x512, other arithmetic, advance(): previous = previous * factor  72.2 us
    all_to_all x2, local copies, waits for them, and re-layouts, local(): lax.all_to_all(lat_spec, 'ang', split_axis=4, concat_axis=0, tiled=True)  70 us
  transfers between devices with their start and end apart: 2, of which 1 were waited for; matrix products, arithmetic and copies ran while one was open for 49% of the time, Pallas kernels for 0%

commit v1 on v0

v1 whole, which is shorter than its diff:
```python
import functools
import math

import jax
import jax.numpy as jnp
from jax import lax
from jax.experimental import pallas as pl
from jax.experimental.pallas import tpu as pltpu
from jax.sharding import PartitionSpec as P

inner_radius = 0.35
rescale_bound = 1e8
rescale_factor = 1e-20
rescale_log = 46.051701859880914
start_log = -1.2051210046670229


def legendre_kernel(chunk, recur_a_ref, recur_ab_ref, orders_ref, log_start_ref, cosines_ref, out_ref, cur_ref, prev_ref, log_ref):
    step_count, slots, lat_count = out_ref.shape
    lanes = recur_a_ref.shape[2]
    tiles = lat_count // lanes
    degree_block = pl.program_id(1)

    @pl.when(degree_block == 0)
    def _():
        cur_ref[...] = jnp.zeros_like(cur_ref)
        prev_ref[...] = jnp.zeros_like(prev_ref)
        log_ref[...] = log_start_ref[...]

    orders = orders_ref[...]

    def run_chunk(index, carry):
        for tile in range(tiles):
            columns = slice(tile * lanes, (tile + 1) * lanes)
            cur, prev, log_scale = cur_ref[:, columns], prev_ref[:, columns], log_ref[:, columns]
            too_large = jnp.abs(cur) > rescale_bound
            factor = jnp.where(too_large, rescale_factor, 1.0)
            log_scale = log_scale + jnp.where(too_large, rescale_log, 0.0)
            cur, prev = cur * factor, prev * factor
            scale = jnp.exp(log_scale)
            cosines = cosines_ref[:, columns]
            for inner in range(chunk):
                step = index * chunk + inner
                starting = orders == degree_block * step_count + step
                grown = recur_a_ref[step] * (cosines * cur) - recur_ab_ref[step] * prev
                cur, prev = jnp.where(starting, 1.0, grown), cur
                out_ref[step, :, columns] = (cur * scale).astype(jnp.bfloat16)
            cur_ref[:, columns] = cur
            prev_ref[:, columns] = prev
            log_ref[:, columns] = log_scale
        return carry

    lax.fori_loop(0, step_count // chunk, run_chunk, 0)


def legendre_rows(orders, degree_count, lat_count):
    slot_count = orders.shape[0]
    lanes, chunk, slot_block, degree_block = 128, 8, 16, 64
    colatitude = (jnp.arange(lat_count, dtype=jnp.float32) + 0.5) * (math.pi / lat_count)
    cosines = jnp.broadcast_to(jnp.cos(colatitude)[None, :], (slot_block, lat_count))
    sines = jnp.sin(colatitude)[None, :]
    order_value = orders.astype(jnp.float32)[:, None]
    log_start = (
        start_log
        + 0.5 * (lax.lgamma(order_value + 1.5) - lax.lgamma(order_value + 1.0))
        + order_value * jnp.log(sines)
    )
    degree_value = jnp.arange(degree_count, dtype=jnp.float32)[:, None]
    order_row = order_value[:, 0][None, :]
    denominator = jnp.maximum(degree_value * degree_value - order_row * order_row, 1.0)
    recur_a = jnp.sqrt(jnp.maximum(4.0 * degree_value * degree_value - 1.0, 1.0) / denominator)
    lower_sq = (degree_value - 1.0) * (degree_value - 1.0)
    recur_b = jnp.sqrt(
        jnp.maximum(lower_sq - order_row * order_row, 0.0) / jnp.maximum(4.0 * lower_sq - 1.0, 1.0)
    )
    table_shape = (degree_count, slot_count, lanes)
    recur_ab = jnp.broadcast_to((recur_a * recur_b)[:, :, None], table_shape)
    recur_a = jnp.broadcast_to(recur_a[:, :, None], table_shape)
    order_tile = jnp.broadcast_to(orders[:, None], (slot_count, lanes))
    table_spec = pl.BlockSpec((degree_block, slot_block, lanes), lambda s, l: (l, s, 0))
    state = pltpu.VMEM((slot_block, lat_count), jnp.float32)
    return pl.pallas_call(
        functools.partial(legendre_kernel, chunk),
        grid=(slot_count // slot_block, degree_count // degree_block),
        in_specs=[
            table_spec,
            table_spec,
            pl.BlockSpec((slot_block, lanes), lambda s, l: (s, 0)),
            pl.BlockSpec((slot_block, lat_count), lambda s, l: (s, 0)),
            pl.BlockSpec((slot_block, lat_count), lambda s, l: (0, 0)),
        ],
        out_specs=pl.BlockSpec((degree_block, slot_block, lat_count), lambda s, l: (l, s, 0)),
        out_shape=jax.ShapeDtypeStruct((degree_count, slot_count, lat_count), jnp.bfloat16),
        scratch_shapes=[state, state, state],
        compiler_params=pltpu.CompilerParams(vmem_limit_bytes=32 * 1024 * 1024),
        cost_estimate=pl.CostEstimate(
            flops=8 * degree_count * slot_count * lat_count,
            bytes_accessed=2 * degree_count * slot_count * (lat_count + 4 * lanes),
            transcendentals=degree_count * slot_count * lat_count // chunk,
        ),
        name="legendre",
    )(recur_a, recur_ab, order_tile, log_start, cosines)


def radial_tables(mode_count, radius_count):
    angles = (jnp.arange(radius_count, dtype=jnp.float32) + 0.5) * (math.pi / radius_count)
    mode_values = jnp.arange(mode_count, dtype=jnp.float32)[:, None]
    values = jnp.cos(mode_values * angles[None, :])
    slopes = (
        mode_values
        * jnp.sin(mode_values * angles[None, :])
        / jnp.sin(angles)[None, :]
        * (2.0 / (1.0 - inner_radius))
    )
    radii = inner_radius + (1.0 - inner_radius) * (jnp.cos(angles) + 1.0) * 0.5
    return jnp.stack([values, slopes + 3.0 * values / radii[None, :]])


def fourier_tables(orders, lon_count):
    phase_index = orders[:, None] * jnp.arange(lon_count, dtype=jnp.int32)[None, :] % lon_count
    phase_angle = phase_index.astype(jnp.float32) * (2.0 * math.pi / lon_count)
    weight = jnp.where(orders == 0, 1.0, 2.0).astype(jnp.float32)[:, None]
    cosine = jnp.cos(phase_angle)
    sine = jnp.sin(phase_angle)
    order_value = orders.astype(jnp.float32)[:, None]
    synth_table = jnp.stack([weight * cosine, -weight * sine], 1).astype(jnp.bfloat16)
    turn_table = jnp.stack(
        [-order_value * weight * sine, -order_value * weight * cosine], 1
    ).astype(jnp.bfloat16)
    analyse_table = (jnp.stack([cosine, -sine], 1) * (2.0 * math.pi / lon_count)).astype(
        jnp.bfloat16
    )
    return (synth_table, turn_table, analyse_table)


def local(source_coeffs, inverses, velocity, order_slots):
    slots_local, degrees_local, _, mode_count = source_coeffs.shape
    lat_local = velocity.shape[1]
    radii_local = velocity.shape[2]
    lon_count = velocity.shape[3]
    rad_count = lax.axis_size("rad")
    ang_count = lax.axis_size("ang")
    degree_count = degrees_local * rad_count
    lat_count = lat_local * ang_count
    radius_count = radii_local * rad_count
    rad_index = lax.axis_index("rad")
    ang_index = lax.axis_index("ang")
    my_orders = lax.dynamic_slice_in_dim(order_slots, ang_index * slots_local, slots_local, 0)
    degrees = rad_index * degrees_local + jnp.arange(degrees_local, dtype=jnp.int32)
    degree_mask = (degrees[None, :] >= my_orders[:, None]).astype(jnp.float32)
    solved = (
        jnp.einsum("lkj,slcj->slck", inverses, source_coeffs, preferred_element_type=jnp.float32)
        * degree_mask[:, :, None, None]
    )
    tables = radial_tables(mode_count, radius_count)
    radial = jnp.einsum("slck,fki->sfcli", solved, tables, precision=lax.Precision.HIGHEST).astype(
        jnp.bfloat16
    )
    radial = lax.all_to_all(radial, "rad", split_axis=4, concat_axis=3, tiled=True)
    legendre = legendre_rows(my_orders, degree_count, lat_count)
    lat_spec = jnp.einsum(
        "sfcli,lsj->sjfci", radial, legendre, preferred_element_type=jnp.float32
    ).astype(jnp.bfloat16)
    lat_spec = lat_spec.reshape(slots_local, lat_count, 4 * radii_local)
    received = lax.all_to_all(lat_spec, "ang", split_axis=1, concat_axis=0, tiled=True)
    slot_count = slots_local * ang_count
    fields = received.reshape(slot_count, lat_local, 2, 2, radii_local)
    synth_table, turn_table, analyse_table = fourier_tables(order_slots, lon_count)
    turn = jnp.einsum(
        "sjci,scn->jin", fields[:, :, 0], turn_table, preferred_element_type=jnp.float32
    )
    growth = jnp.einsum(
        "sjci,scn->jin", fields[:, :, 1], synth_table, preferred_element_type=jnp.float32
    )
    lat_rows = ang_index * lat_local + jnp.arange(lat_local, dtype=jnp.int32)
    colatitude = (lat_rows.astype(jnp.float32) + 0.5) * (math.pi / lat_count)
    sines = jnp.sin(colatitude)
    quad_weight = math.pi / lat_count * sines
    radius_rows = rad_index * radii_local + jnp.arange(radii_local, dtype=jnp.int32)
    angles = (radius_rows.astype(jnp.float32) + 0.5) * (math.pi / radius_count)
    radius_col = (inner_radius + (1.0 - inner_radius) * (jnp.cos(angles) + 1.0) * 0.5)[
        None, :, None
    ]
    flux_term = velocity[0].astype(jnp.float32) * growth + velocity[1].astype(jnp.float32) * (
        turn / (radius_col * sines[:, None, None])
    )
    flux_term = flux_term.astype(jnp.bfloat16).reshape(lat_local * radii_local, lon_count)
    analyse_table = analyse_table.reshape(slot_count * 2, lon_count)
    fourier = jnp.einsum("qn,pn->pq", flux_term, analyse_table, preferred_element_type=jnp.float32)
    weight_row = jnp.repeat(quad_weight, radii_local)
    fourier = (fourier * weight_row[None, :]).astype(jnp.bfloat16)
    fourier = lax.all_to_all(fourier, "ang", split_axis=0, concat_axis=1, tiled=True)
    fourier = fourier.reshape(slots_local, 2, lat_count, radii_local)
    advected = jnp.einsum(
        "scji,lsj->scil", fourier, legendre, preferred_element_type=jnp.float32
    ).astype(jnp.bfloat16)
    return advected


def solution(mesh):
    in_specs = (P("ang", "rad", None, None), P("rad", None, None), P(None, "ang", "rad", None), P())
    out_specs = P("ang", None, "rad", None)
    return jax.shard_map(local, mesh=mesh, in_specs=in_specs, out_specs=out_specs, check_vma=False)
```

time: 2500 us -> 905 us (0.36)
  other arithmetic: 912 us -> 19.2 us
  local copies, waits for them, and re-layouts: 598 us -> 177 us
  loops' own time: 316 us -> 0 us
  blocking collectives: 189 us -> 142 us
  waiting for transfers between devices: 243 us -> 288 us
  Pallas kernels: 0 us -> 42.8 us
    dynamic_update_slice x512 -> x0, other arithmetic: 456 us -> none  [legendre_rows(): lax.scan(advance, (zero_field, zero_field, log_start), jnp.arange(degree_...]
    another operation x1 -> x0, loops' own time: 316 us -> none  [legendre_rows(): lax.scan(advance, (zero_field, zero_field, log_start), jnp.arange(degree_...]
    dynamic_slice x512 -> x0, local copies, waits for them, and re-layouts: 302 us -> none  [legendre_rows(): lax.scan(advance, (zero_field, zero_field, log_start), jnp.arange(degree_...]
    or x512 -> x0, other arithmetic: 289 us -> none  [advance(): previous = jnp.where(before | starting, 0.0, prev_one)]
    cos x513 -> x1, other arithmetic: 79.6 us -> 0.05 us  [legendre_rows(): jnp.cos(colatitude)[None, :]]
    all_to_all x4 -> x2, local copies, waits for them, and re-layouts: 107 us -> 27.6 us  [the longest x1 21.4 us: local(): lax.all_to_all(lat_spec, 'ang', split_axis=1, concat_axis=0, tiled=True)]
    mul x514 -> x4, other arithmetic: 73 us -> 0.19 us  [the longest x1 0.17 us: legendre_rows(): recur_ab = jnp.broadcast_to((recur_a * recur_b)[:, :, None], table_shape)]
    convert_element_type x2 -> x3, local copies, waits for them, and re-layouts: 57.1 us -> 6.01 us  [the longest x2 5.91 us: fourier_tables(): (jnp.stack([cosine, -sine], 1) * (2.0 * math.pi / lon_count)).astype(jnp....]
  transfers between devices with their start and end apart: 2 -> 2, of which waited for: 1 -> 2; matrix products, arithmetic and copies ran while one was open for 49% -> 4% of each run, Pallas kernels for 0% -> 5%
where the time goes in v1:
time: 905 us; the launch traced here: 894 us
  waiting for transfers between devices  288 us (32%)
  matrix products  211 us (23%)
  local copies, waits for them, and re-layouts  177 us (20%)
  blocking collectives  142 us (16%)
  Pallas kernels  42.8 us (5%)
  other arithmetic  19.2 us (2%)
  starting transfers between devices  13 us (1%)
    all_to_all x1, waiting for transfers between devices, local(): lax.all_to_all(lat_spec, 'ang', split_axis=1, concat_axis=0, tiled=True)  249 us
    all_to_all x1, blocking collectives, local(): lax.all_to_all(fourier, 'ang', split_axis=0, concat_axis=1, tiled=True)  142 us
    dot_general x1, matrix products, local(): jnp.einsum('scji,lsj->scil', fourier, legendre, preferred_element_type=jn...  82.1 us
    dot_general x1, matrix products, local(): jnp.einsum('sfcli,lsj->sjfci', radial, legendre, preferred_element_type=j...  48.3 us
    pallas_call x1, Pallas kernels, legendre_rows(): pl.pallas_call(functools.partial(legendre_kernel, chunk), grid=(slot_coun...  42.8 us
    all_to_all x1, waiting for transfers between devices, local(): lax.all_to_all(radial, 'rad', split_axis=4, concat_axis=3, tiled=True)  38.7 us
    unnamed x6, local copies, waits for them, and re-layouts  30.4 us
    reshape x1, local copies, waits for them, and re-layouts, local(): fourier = fourier.reshape(slots_local, 2, lat_count, radii_local)  27.8 us
  transfers between devices with their start and end apart: 2, of which 2 were waited for; matrix products, arithmetic and copies ran while one was open for 4% of the time, Pallas kernels for 5%

profile of v1, /device:TPU:0, one launch (start us, length us, event | category | flops | bytes accessed | tf_op | source)
XLA Modules:
  0.0 893.8 jit_solution(9768685310929476075)
XLA Ops:
  0.1 0.8 multiply_add_fusion.3
  1.0 0.1 compare_convert_fusion
  1.0 0.1 copy.37
  1.1 6.9 bitcast_multiply_fusion
  8.0 0.3 fusion.42
  8.3 21.1 %convert_bitcast_fusion = bf16[64,2,2,128,128]{3,4,2,0,1:T(8,128)(2,1)S(1)} fusion(f32[64,128,2,128]{3,0,2,1:T(8,128)S(1)} %bitcast_multiply_fusion, f32[1,128,128]{1,2,0:T(8,128)S(1)} %get-tuple-element.21, f32[1,128,128]{1,2,0:T(8,128)S(1)} %get-tuple-element.20), kind=kOutput, calls=%fused_computation.15 | convolution fusion | flops 6446678016 | bytes 16908288 | tf_op jit(solution)/shard_map/slck,fki->sfcli/dot_general | solution.py:156
  29.4 18.7 %copy.39 = bf16[64,2,2,128,128]{3,2,0,1,4:T(2,128)(2,1)} copy(bf16[64,2,2,128,128]{3,4,2,0,1:T(8,128)(2,1)S(1)} %convert_bitcast_fusion) | data formatting | bytes 16777216 | tf_op jit(solution)/shard_map/convert_element_type | solution.py:156
  48.1 5.8 all-to-all-start
  54.0 0.2 sqrt_multiply_fusion
  54.2 0.1 copy.34
  54.3 0.1 copy.35
  54.5 0.1 multiply_add_fusion.log_start_ref
  54.6 4.6 broadcast_in_dim.14.recur_a_ref
  59.2 7.0 broadcast_in_dim.15.recur_ab_ref
  66.3 0.1 broadcast_in_dim.16.orders_ref
  66.3 42.8 %legendre.1 = bf16[512,64,768]{2,1,0:T(8,128)(2,1)} custom-call(f32[512,64,128]{2,1,0:T(8,128)S(1)} %broadcast_in_dim.14.recur_a_ref, f32[512,64,128]{2,1,0:T(8,128)} %broadcast_in_dim.15.recur_ab_ref, s32[64,128]{1,0:T(8,128)S(1)} %broadcast_in_dim.16.orders_ref, f32[64,768]{1,0:T(8,128)S(1)} %multiply_add_fusion.log_start_ref, ...), custom_call_target="tpu_custom_call" | custom-call | flops 201326592 | bytes 83886080 | tf_op jit(solution)/shard_map/legendre/pallas_call | solution.py:82
  109.1 38.7 %all-to-all-done = bf16[64,2,2,128,128]{3,2,0,1,4:T(2,128)(2,1)} async-done(((bf16[64,2,2,128,128]{3,2,0,1,4:T(2,128)(2,1)}), bf16[64,2,2,128,128]{3,2,0,1,4:T(2,128)(2,1)}, u32[]{:S(2)}, u32[]{:S(2)}) %all-to-all-start) | async-done | bytes 8388640 | tf_op jit(solution)/shard_map/all_to_all | solution.py:159
  147.8 12.2 %copy.83 = bf16[64,2,2,128,4,32]{3,4,5,2,1,0:T(4,128)(2,1)} copy(bf16[64,2,2,128,4,32]{3,2,0,1,5,4:T(2,128)(2,1)} %bitcast.9) | data formatting | bytes 16777216 | tf_op jit(solution)/shard_map/all_to_all | solution.py:159
  159.9 13.1 %all_to_all.39 = bf16[64,2,2,512,32]{3,4,2,1,0:T(8,128)(2,1)} reshape(bf16[64,2,2,4,128,32]{4,3,5,2,1,0:T(4,128)(2,1)} %bitcast.70) | data formatting | bytes 16777216 | tf_op jit(solution)/shard_map/all_to_all | solution.py:159
  173.1 48.3 %fusion.9 = bf16[64,768,2,2,32]{1,4,3,2,0:T(8,128)(2,1)} fusion(bf16[64,2,2,512,32]{3,4,2,1,0:T(8,128)(2,1)} %all_to_all.39, bf16[512,64,768,1,1]{2,1,0,4,3:T(8,128)(2,1)} %bitcast.68), kind=kOutput, calls=%fused_computation.16 | convolution fusion | flops 6448742400 | bytes 71303168 | tf_op jit(solution)/shard_map/sfcli,lsj->sjfci/dot_general | solution.py:161
  221.3 16.7 %copy.42 = bf16[64,768,128]{2,0,1:T(8,128)(2,1)} copy(bf16[64,768,128]{1,2,0:T(8,128)(2,1)} %bitcast.72) | data formatting | bytes 25165824 | tf_op jit(solution)/shard_map/reshape | solution.py:164
  238.0 0.0 copy-start.1
  238.0 7.2 all-to-all-start.1
  245.2 0.0 copy-done.1
  245.3 16.4 %multiply_convert_fusion.2 = (bf16[512,1,1536]{2,0,1:T(8,128)(2,1)}, bf16[512,1,1536]{2,0,1:T(8,128)(2,1)}, bf16[512,1,1536]{2,0,1:T(8,128)(2,1)}, bf16[512,1,15...) fusion(f32[512]{0:T(512)S(1)} %get-tuple-element.17, s32[512]{0:T(512)S(1)} %copy-done.1, ...), kind=kLoop, calls=%fused_computation.35 | loop fusion | flops 14155776 | bytes 12591104 | tf_op jit(solution)/shard_map/convert.2
  261.7 0.9 fusion.12
  262.5 3.2 copy.33
  265.8 2.7 convert_element_type.104
  268.5 0.1 broadcast_in_dim.19
  268.6 0.1 mul.489
  268.7 0.1 multiply_add_fusion.1
  268.7 0.1 broadcast_multiply_fusion
  268.8 249.2 %all-to-all-done.1 = bf16[64,768,128]{2,0,1:T(8,128)(2,1)} async-done(((bf16[64,768,128]{2,0,1:T(8,128)(2,1)}), bf16[64,768,128]{2,0,1:T(8,128)(2,1)}, u32[]{:S(2)}, u32[]{:S(2)}) %all-to-all-start.1) | async-done | bytes 12582944 | tf_op jit(solution)/shard_map/all_to_all | solution.py:165
  518.0 21.4 %copy.44 = bf16[8,64,96,128]{2,3,1,0:T(8,128)(2,1)} copy(bf16[8,64,96,128]{3,1,2,0:T(8,128)(2,1)} %bitcast.14) | data formatting | bytes 25165824 | tf_op jit(solution)/shard_map/all_to_all | solution.py:165
  539.4 12.9 %fusion.57 = (bf16[512,96,1,2,32]{1,4,3,2,0:T(8,128)(2,1)}, bf16[512,96,1,2,32]{1,4,3,2,0:T(8,128)(2,1)}) fusion(bf16[512,96,2,2,32]{1,4,3,2,0:T(8,128)(2,1)} %bitcast.67), kind=kLoop, calls=%fused_computation.115 | loop fusion | bytes 25165824 | tf_op jit(solution)/shard_map/slice | solution.py:170
  552.3 15.1 %copy.62 = bf16[512,96,1,2,32]{0,4,3,1,2:T(8,128)(2,1)} copy(bf16[512,96,1,2,32]{1,4,3,2,0:T(8,128)(2,1)} %get-tuple-element.8) | data formatting | bytes 12582912
  567.4 15.2 %copy.63 = bf16[512,96,1,2,32]{0,4,3,1,2:T(8,128)(2,1)} copy(bf16[512,96,1,2,32]{1,4,3,2,0:T(8,128)(2,1)} %get-tuple-element.7) | data formatting | bytes 12582912
  582.7 0.0 copy-start
  582.7 16.9 %fusion.14 = f32[96,32,1536,1]{2,1,3,0:T(8,128)} fusion(bf16[512,96,1,2,32]{0,4,3,1,2:T(8,128)(2,1)} %copy.62, bf16[512,1,1536]{2,0,1:T(8,128)(2,1)} %get-tuple-element.14, bf16[512,1,1536]{2,0,1:T(8,128)(2,1)} %get-tuple-element.13), kind=kOutput, calls=%fused_computation.20 | convolution fusion | flops 9665249280 | bytes 28311552 | tf_op jit(solution)/shard_map/sjci,scn->jin/dot_general | solution.py:172
  599.5 0.0 copy-done
  599.5 22.5 %fusion.5 = bf16[96,32,1536]{2,1,0:T(8,128)(2,1)} fusion(f32[96,32,1536,1]{2,1,3,0:T(8,128)} %fusion.14, f32[96,32]{1,0:T(8,128)S(1)} %broadcast_multiply_fusion, bf16[2,96,32,1536]{3,2,1,0:T(8,128)(2,1)} %param.6, bf16[512,96,1,2,32]{0,4,3,1,2:T(8,128)(2,1)S(1)} %copy-done, bf16[512,1,1536]{2,0,1:T(8,128)(2,1)} %get-tuple-element.12, ...), kind=kOutput, calls=%fused_computation.6 | convolution fusion | flops 9698279424 | bytes 56635392 | tf_op jit(solution)/shard_map/sjci,scn->jin/dot_general | solution.py:169
  622.0 13.5 %multiply_convert_fusion = bf16[1024,3072]{1,0:T(8,128)(2,1)S(1)} fusion(bf16[1024,1536]{1,0:T(8,128)(2,1)} %convert_element_type.104, bf16[3072,1536]{1,0:T(8,128)(2,1)} %bitcast.74, f32[3072]{0:T(1024)S(1)} %mul.489), kind=kOutput, calls=%fused_computation.9 | convolution fusion | flops 9669967872 | bytes 18886656 | tf_op jit(solution)/shard_map/qn,pn->pq/dot_general | solution.py:189
  635.5 141.7 %all_to_all.49 = bf16[8,128,3072]{2,1,0:T(8,128)(2,1)S(1)} all-to-all(bf16[8,128,3072]{2,1,0:T(8,128)(2,1)S(1)} %bitcast.73), channel_id=1, replica_groups=mesh['rad'=4,'ang'=8] {'ang'}, dimensions={0} | all-to-all | bytes 12582912 | tf_op jit(solution)/shard_map/all_to_all | solution.py:192
  777.2 6.2 copy.47
  783.4 27.8 %reshape.782 = bf16[64,2,768,32]{3,2,1,0:T(8,128)(2,1)} reshape(bf16[128,8,3072]{2,1,0:T(8,128)(2,1)} %copy.47) | data formatting | bytes 12582912 | tf_op jit(solution)/shard_map/reshape | solution.py:193
  811.3 82.1 %fusion.37 = bf16[64,2,32,512]{3,2,1,0:T(8,128)(2,1)} fusion(bf16[64,2,768,32]{3,2,1,0:T(8,128)(2,1)} %reshape.782, bf16[512,64,768,1]{2,1,0,3:T(8,128)(2,1)} %bitcast.69), kind=kOutput, calls=%fused_computation.45 | convolution fusion | flops 3223322624 | bytes 60817408 | tf_op jit(solution)/shard_map/scji,lsj->scil/dot_general | solution.py:194
  (12 shorter events, 0.3 us)
Async XLA Ops:
  48.1 99.7 %all-to-all-start = ((bf16[64,2,2,128,128]{3,2,0,1,4:T(2,128)(2,1)}), bf16[64,2,2,128,128]{3,2,0,1,4:T(2,128)(2,1)}, u32[]{:S(2)}, u32[]{:S(2)}) async-start(bf16[64,2,2,128,128]{3,2,0,1,4:T(2,128)(2,1)} %copy.39), calls=%async_computation | async-start | bytes 16777216 | tf_op jit(solution)/shard_map/all_to_all | solution.py:159
  238.0 7.2 copy-start.1
  238.0 280.0 %all-to-all-start.1 = ((bf16[64,768,128]{2,0,1:T(8,128)(2,1)}), bf16[64,768,128]{2,0,1:T(8,128)(2,1)}, u32[]{:S(2)}, u32[]{:S(2)}) async-start(bf16[64,768,128]{2,0,1:T(8,128)(2,1)} %copy.42), calls=%async_computation.1 | async-start | bytes 25165824 | tf_op jit(solution)/shard_map/all_to_all | solution.py:165
  582.7 16.9 %copy-start = (bf16[512,96,1,2,32]{0,4,3,1,2:T(8,128)(2,1)S(1)}, bf16[512,96,1,2,32]{0,4,3,1,2:T(8,128)(2,1)}, u32[]{:S(2)}) copy-start(bf16[512,96,1,2,32]{0,4,3,1,2:T(8,128)(2,1)} %copy.63) | copy-start | bytes 18874372

commit v2 on v1

--- a/solution.py
+++ b/solution.py
@@ -157,21 +157,30 @@
         jnp.bfloat16
     )
     radial = lax.all_to_all(radial, "rad", split_axis=4, concat_axis=3, tiled=True)
-    legendre = legendre_rows(my_orders, degree_count, lat_count)
-    lat_spec = jnp.einsum(
-        "sfcli,lsj->sjfci", radial, legendre, preferred_element_type=jnp.float32
-    ).astype(jnp.bfloat16)
-    lat_spec = lat_spec.reshape(slots_local, lat_count, 4 * radii_local)
-    received = lax.all_to_all(lat_spec, "ang", split_axis=1, concat_axis=0, tiled=True)
-    slot_count = slots_local * ang_count
-    fields = received.reshape(slot_count, lat_local, 2, 2, radii_local)
-    synth_table, turn_table, analyse_table = fourier_tables(order_slots, lon_count)
-    turn = jnp.einsum(
-        "sjci,scn->jin", fields[:, :, 0], turn_table, preferred_element_type=jnp.float32
-    )
-    growth = jnp.einsum(
-        "sjci,scn->jin", fields[:, :, 1], synth_table, preferred_element_type=jnp.float32
-    )
+    parts = 2
+    part_slots = slots_local // parts
+    slot_count = part_slots * ang_count
+    grouped_orders = order_slots.reshape(ang_count, parts, part_slots)
+    legendre, received, tables_of = [], [], []
+    for part in range(parts):
+        own = slice(part * part_slots, (part + 1) * part_slots)
+        legendre.append(legendre_rows(my_orders[own], degree_count, lat_count))
+        lat_spec = jnp.einsum(
+            "sfcli,lsj->sjfci", radial[own], legendre[part], preferred_element_type=jnp.float32
+        ).astype(jnp.bfloat16)
+        lat_spec = lat_spec.reshape(part_slots, lat_count, 4 * radii_local)
+        received.append(lax.all_to_all(lat_spec, "ang", split_axis=1, concat_axis=0, tiled=True))
+        tables_of.append(fourier_tables(grouped_orders[:, part].reshape(-1), lon_count))
+    turn, growth = 0.0, 0.0
+    for part in range(parts):
+        fields = received[part].reshape(slot_count, lat_local, 2, 2, radii_local)
+        synth_table, turn_table, _ = tables_of[part]
+        turn += jnp.einsum(
+            "sjci,scn->jin", fields[:, :, 0], turn_table, preferred_element_type=jnp.float32
+        )
+        growth += jnp.einsum(
+            "sjci,scn->jin", fields[:, :, 1], synth_table, preferred_element_type=jnp.float32
+        )
     lat_rows = ang_index * lat_local + jnp.arange(lat_local, dtype=jnp.int32)
     colatitude = (lat_rows.astype(jnp.float32) + 0.5) * (math.pi / lat_count)
     sines = jnp.sin(colatitude)
@@ -185,16 +194,25 @@
         turn / (radius_col * sines[:, None, None])
     )
     flux_term = flux_term.astype(jnp.bfloat16).reshape(lat_local * radii_local, lon_count)
-    analyse_table = analyse_table.reshape(slot_count * 2, lon_count)
-    fourier = jnp.einsum("qn,pn->pq", flux_term, analyse_table, preferred_element_type=jnp.float32)
     weight_row = jnp.repeat(quad_weight, radii_local)
-    fourier = (fourier * weight_row[None, :]).astype(jnp.bfloat16)
-    fourier = lax.all_to_all(fourier, "ang", split_axis=0, concat_axis=1, tiled=True)
-    fourier = fourier.reshape(slots_local, 2, lat_count, radii_local)
-    advected = jnp.einsum(
-        "scji,lsj->scil", fourier, legendre, preferred_element_type=jnp.float32
-    ).astype(jnp.bfloat16)
-    return advected
+    exchanged = []
+    for part in range(parts):
+        analyse_table = tables_of[part][2].reshape(slot_count * 2, lon_count)
+        fourier = jnp.einsum(
+            "qn,pn->pq", flux_term, analyse_table, preferred_element_type=jnp.float32
+        )
+        fourier = (fourier * weight_row[None, :]).astype(jnp.bfloat16)
+        exchanged.append(lax.all_to_all(fourier, "ang", split_axis=0, concat_axis=1, tiled=True))
+    advected = []
+    for part in range(parts):
+        fourier = exchanged[part].reshape(part_slots, 2, lat_count, radii_local)
+        fourier = lax.optimization_barrier(fourier.transpose(0, 1, 3, 2))
+        advected.append(
+            jnp.einsum(
+                "scij,lsj->scil", fourier, legendre[part], preferred_element_type=jnp.float32
+            ).astype(jnp.bfloat16)
+        )
+    return jnp.concatenate(advected, 0)
 
 
 def solution(mesh):

time: 905 us -> 878 us (0.970)
  blocking collectives: 142 us -> 0 us
  waiting for transfers between devices: 288 us -> 340 us
  matrix products: 211 us -> 247 us
  local copies, waits for them, and re-layouts: 177 us -> 191 us
  starting transfers between devices: 13 us -> 26 us
    all_to_all x1 -> x0, blocking collectives: 142 us -> none  [local(): lax.all_to_all(fourier, 'ang', split_axis=0, concat_axis=1, tiled=True)]
    all_to_all x0 -> x2, waiting for transfers between devices: none -> 118 us  [local(): lax.all_to_all(fourier, 'ang', split_axis=0, concat_axis=1, tiled=True)]
    all_to_all x1 -> x2, waiting for transfers between devices: 249 us -> 153 us  [local(): lax.all_to_all(lat_spec, 'ang', split_axis=1, concat_axis=0, tiled=True)]
    all_to_all x1, waiting for transfers between devices: 38.7 us -> 68.5 us  [local(): lax.all_to_all(radial, 'rad', split_axis=4, concat_axis=3, tiled=True)]
    slice x0 -> x5, local copies, waits for them, and re-layouts: none -> 26.4 us  [the longest x3 19.8 us: local(): radial[own]]
    dot_general x1 -> x2, matrix products: 22.5 us -> 40.5 us  [local(): jnp.einsum('sjci,scn->jin', fields[:, :, 0], turn_table, preferred_elemen...]
    all_to_all x2 -> x1, local copies, waits for them, and re-layouts: 25.3 us -> 10.1 us  [local(): lax.all_to_all(radial, 'rad', split_axis=4, concat_axis=3, tiled=True)]
    dot_general x2 -> x4, matrix products: 130 us -> 142 us  [the longest x2 87.2 us: local(): jnp.einsum('scij,lsj->scil', fourier, legendre[part], preferred_element_t...]
  transfers between devices with their start and end apart: 2 -> 5, of which waited for: 2 -> 5; matrix products, arithmetic and copies ran while one was open for 4% -> 15% of each run, Pallas kernels for 5% -> 4%
where the time goes in v2:
time: 878 us; the launch traced here: 869 us
  waiting for transfers between devices  340 us (39%)
  matrix products  247 us (28%)
  local copies, waits for them, and re-layouts  191 us (22%)
  Pallas kernels  38.9 us (4%)
  starting transfers between devices  26 us (3%)
  other arithmetic  25.2 us (3%)
    all_to_all x2, waiting for transfers between devices, local(): lax.all_to_all(lat_spec, 'ang', split_axis=1, concat_axis=0, tiled=True)  153 us
    all_to_all x2, waiting for transfers between devices, local(): lax.all_to_all(fourier, 'ang', split_axis=0, concat_axis=1, tiled=True)  118 us
    dot_general x2, matrix products, local(): jnp.einsum('scij,lsj->scil', fourier, legendre[part], preferred_element_t...  87.2 us
    all_to_all x1, waiting for transfers between devices, local(): lax.all_to_all(radial, 'rad', split_axis=4, concat_axis=3, tiled=True)  68.5 us
    dot_general x2, matrix products, local(): jnp.einsum('sfcli,lsj->sjfci', radial[own], legendre[part], preferred_ele...  54.4 us
    dot_general x2, matrix products, local(): jnp.einsum('sjci,scn->jin', fields[:, :, 0], turn_table, preferred_elemen...  40.5 us
    pallas_call x2, Pallas kernels, legendre_rows(): pl.pallas_call(functools.partial(legendre_kernel, chunk), grid=(slot_coun...  38.9 us
    unnamed x20, local copies, waits for them, and re-layouts  31.5 us
  transfers between devices with their start and end apart: 5, of which 5 were waited for; matrix products, arithmetic and copies ran while one was open for 15% of the time, Pallas kernels for 4%

profile of v2, /device:TPU:0, one launch (start us, length us, event | category | flops | bytes accessed | tf_op | source)
XLA Modules:
  0.0 868.8 jit_solution(11105383701996287754)
XLA Ops:
  1.3 6.9 bitcast_multiply_fusion
  8.2 21.1 %convert_bitcast_fusion = bf16[64,2,2,128,128]{3,4,2,0,1:T(8,128)(2,1)S(1)} fusion(f32[64,128,2,128]{3,0,2,1:T(8,128)S(1)} %bitcast_multiply_fusion, f32[1,128,128]{1,2,0:T(8,128)S(1)} %get-tuple-element.48, f32[1,128,128]{1,2,0:T(8,128)S(1)} %get-tuple-element.47), kind=kOutput, calls=%fused_computation.20 | convolution fusion | flops 6446678016 | bytes 16908288 | tf_op jit(solution)/shard_map/slck,fki->sfcli/dot_general | solution.py:156
  29.3 18.7 %copy.60 = bf16[64,2,2,128,128]{3,2,0,1,4:T(2,128)(2,1)} copy(bf16[64,2,2,128,128]{3,4,2,0,1:T(8,128)(2,1)S(1)} %convert_bitcast_fusion) | data formatting | bytes 16777216 | tf_op jit(solution)/shard_map/convert_element_type | solution.py:156
  48.0 5.9 all-to-all-start
  59.5 19.6 %legendre.3 = bf16[512,32,768]{2,1,0:T(8,128)(2,1)} custom-call(f32[512,32,128]{2,1,0:T(8,128)S(1)} %broadcast_in_dim.34.recur_a_ref, f32[512,32,128]{2,1,0:T(8,128)S(1)} %broadcast_in_dim.35.recur_ab_ref, s32[32,128]{1,0:T(8,128)S(1)} %broadcast_in_dim.36.orders_ref, f32[32,768]{1,0:T(8,128)S(1)} %get-tuple-element.17.log_start_ref, ...), custom_call_target="tpu_custom_call" | custom-call | flops 100663296 | bytes 41943040 | tf_op jit(solution)/shard_map/legendre/pallas_call | solution.py:82
  79.1 68.5 %all-to-all-done = bf16[64,2,2,128,128]{3,2,0,1,4:T(2,128)(2,1)} async-done(((bf16[64,2,2,128,128]{3,2,0,1,4:T(2,128)(2,1)}), bf16[64,2,2,128,128]{3,2,0,1,4:T(2,128)(2,1)}, u32[]{:S(2)}, u32[]{:S(2)}) %all-to-all-start) | async-done | bytes 8388640 | tf_op jit(solution)/shard_map/all_to_all | solution.py:159
  147.6 10.1 %copy.136 = bf16[64,2,2,128,4,32]{3,4,5,2,1,0:T(4,128)(2,1)S(1)} copy(bf16[64,2,2,128,4,32]{3,2,0,1,5,4:T(2,128)(2,1)} %bitcast.9) | data formatting | bytes 16777216 | tf_op jit(solution)/shard_map/all_to_all | solution.py:159
  157.7 5.4 fusion.96
  163.1 7.2 slice.50
  170.3 27.1 %fusion.22 = bf16[32,768,2,2,32]{1,4,3,2,0:T(8,128)(2,1)} fusion(bf16[32,2,2,512,32]{3,4,2,1,0:T(8,128)(2,1)} %slice.50, bf16[512,32,768,1,1]{2,1,0,4,3:T(8,128)(2,1)} %bitcast.109), kind=kOutput, calls=%fused_computation.28 | convolution fusion | flops 3224371200 | bytes 35651584 | tf_op jit(solution)/shard_map/sfcli,lsj->sjfci/dot_general | solution.py:168
  197.4 9.4 %copy.70 = bf16[32,768,128]{2,0,1:T(8,128)(2,1)} copy(bf16[32,768,128]{1,2,0:T(8,128)(2,1)} %bitcast.116) | data formatting | bytes 12582912 | tf_op jit(solution)/shard_map/reshape | solution.py:171
  206.9 6.7 all-to-all-start.2
  218.5 19.3 %legendre.2 = bf16[512,32,768]{2,1,0:T(8,128)(2,1)} custom-call(f32[512,32,128]{2,1,0:T(8,128)S(1)} %broadcast_in_dim.26.recur_a_ref, f32[512,32,128]{2,1,0:T(8,128)S(1)} %broadcast_in_dim.27.recur_ab_ref, s32[32,128]{1,0:T(8,128)S(1)} %broadcast_in_dim.28.orders_ref, f32[32,768]{1,0:T(8,128)S(1)} %get-tuple-element.18.log_start_ref, ...), custom_call_target="tpu_custom_call" | custom-call | flops 100663296 | bytes 41943040 | tf_op jit(solution)/shard_map/legendre/pallas_call | solution.py:82
  237.8 7.2 slice.46
  244.9 27.3 %fusion.19 = bf16[32,768,2,2,32]{1,4,3,2,0:T(8,128)(2,1)} fusion(bf16[32,2,2,512,32]{3,4,2,1,0:T(8,128)(2,1)} %slice.46, bf16[512,32,768,1,1]{2,1,0,4,3:T(8,128)(2,1)} %bitcast.111), kind=kOutput, calls=%fused_computation.27 | convolution fusion | flops 3224371200 | bytes 35651584 | tf_op jit(solution)/shard_map/sfcli,lsj->sjfci/dot_general | solution.py:168
  272.3 9.0 %copy.63 = bf16[32,768,128]{2,0,1:T(8,128)(2,1)} copy(bf16[32,768,128]{1,2,0:T(8,128)(2,1)} %bitcast.117) | data formatting | bytes 12582912 | tf_op jit(solution)/shard_map/reshape | solution.py:171
  281.3 70.3 %all-to-all-done.2 = bf16[32,768,128]{2,0,1:T(8,128)(2,1)} async-done(((bf16[32,768,128]{2,0,1:T(8,128)(2,1)}), bf16[32,768,128]{2,0,1:T(8,128)(2,1)}, u32[]{:S(2)}, u32[]{:S(2)}) %all-to-all-start.2) | async-done | bytes 6291488 | tf_op jit(solution)/shard_map/all_to_all | solution.py:172
  351.6 4.9 all-to-all-start.1
  357.0 8.5 multiply_convert_fusion.3
  369.1 8.8 %fusion.64 = (f32[256,1,1536]{2,0,1:T(8,128)}, bf16[256,1,1536]{2,0,1:T(8,128)(2,1)}, bf16[256,1,1536]{2,0,1:T(8,128)(2,1)}, f32[256,1,1536]{2,0,1:T(8,128)}, bf...) fusion(s32[256]{0:T(256)S(1)} %mul.633, f32[256]{0:T(256)S(1)} %get-tuple-element.36, ...), kind=kLoop, calls=%fused_computation.78 | loop fusion | flops 7077888 | bytes 6295552 | tf_op jit(solution)/shard_map/cos | solution.py:123
  377.9 11.5 %copy.72 = bf16[8,32,96,128]{2,3,1,0:T(8,128)(2,1)} copy(bf16[8,32,96,128]{3,1,2,0:T(8,128)(2,1)} %bitcast.24) | data formatting | bytes 12582912 | tf_op jit(solution)/shard_map/all_to_all | solution.py:172
  389.4 6.6 fusion.94
  396.1 7.0 copy.108
  403.1 8.2 copy.106
  411.3 82.5 %all-to-all-done.1 = bf16[32,768,128]{2,0,1:T(8,128)(2,1)} async-done(((bf16[32,768,128]{2,0,1:T(8,128)(2,1)}), bf16[32,768,128]{2,0,1:T(8,128)(2,1)}, u32[]{:S(2)}, u32[]{:S(2)}) %all-to-all-start.1) | async-done | bytes 6291488 | tf_op jit(solution)/shard_map/all_to_all | solution.py:172
  493.8 11.5 %copy.65 = bf16[8,32,96,128]{2,3,1,0:T(8,128)(2,1)} copy(bf16[8,32,96,128]{3,1,2,0:T(8,128)(2,1)} %bitcast.14) | data formatting | bytes 12582912 | tf_op jit(solution)/shard_map/all_to_all | solution.py:172
  505.3 6.6 fusion.95
  511.9 8.2 copy.105
  520.0 8.1 copy.107
  528.2 11.1 %fusion.32 = f32[96,32,1536,1]{2,1,3,0:T(8,128)} fusion(bf16[256,96,1,2,32]{0,4,3,1,2:T(8,128)(2,1)} %copy.107, bf16[256,1,1536]{2,0,1:T(8,128)(2,1)} %get-tuple-element.27, bf16[256,1,1536]{2,0,1:T(8,128)(2,1)} %get-tuple-element.28), kind=kOutput, calls=%fused_computation.34 | convolution fusion | flops 4832624640 | bytes 23592960 | tf_op jit(solution)/shard_map/sjci,scn->jin/dot_general | solution.py:178
  539.3 9.4 %fusion.36 = f32[96,32,1536,1]{2,1,3,0:T(8,128)} fusion(bf16[256,96,1,2,32]{0,4,3,1,2:T(8,128)(2,1)S(1)} %copy-done.2, bf16[256,1,1536]{2,0,1:T(8,128)(2,1)S(1)} %copy-done.6, bf16[256,1,1536]{2,0,1:T(8,128)(2,1)S(1)} %copy-done.5), kind=kOutput, calls=%fused_computation.38 | convolution fusion | flops 4832624640 | bytes 23592960 | tf_op jit(solution)/shard_map/sjci,scn->jin/dot_general | solution.py:181
  548.7 9.2 %fusion.34 = f32[96,32,1536,1]{2,1,3,0:T(8,128)} fusion(bf16[256,96,1,2,32]{0,4,3,1,2:T(8,128)(2,1)S(1)} %copy-done.1, bf16[256,1,1536]{2,0,1:T(8,128)(2,1)S(1)} %copy-done.4, bf16[256,1,1536]{2,0,1:T(8,128)(2,1)S(1)} %copy-done.3), kind=kOutput, calls=%fused_computation.36 | convolution fusion | flops 4832624640 | bytes 23592960 | tf_op jit(solution)/shard_map/sjci,scn->jin/dot_general | solution.py:181
  557.9 29.4 %fusion.9 = bf16[96,32,1536]{2,1,0:T(8,128)(2,1)} fusion(f32[96,32,1536,1]{2,1,3,0:T(8,128)} %fusion.32, f32[96,32,1536,1]{2,1,3,0:T(8,128)} %fusion.34, f32[96,32,1536,1]{2,1,3,0:T(8,128)} %fusion.36, f32[96,32]{1,0:T(8,128)S(1)} %broadcast_multiply_fusion, bf16[2,96,32,1536]{3,2,1,0:T(8,128)(2,1)} %param.6, bf16[256,96,1,2,32]{0,4,3,1,2:T(8,128)(2,1)S(1)} %copy.108, ...), kind=kOutput, calls=%fused_computation.10 | convolution fusion | flops 4875091968 | bytes 89665536 | tf_op jit(solution)/shard_map/sjci,scn->jin/dot_general | solution.py:178
  587.3 9.3 %multiply_convert_fusion = bf16[512,3072]{1,0:T(8,128)(2,1)} fusion(bf16[512,1536]{1,0:T(8,128)(2,1)} %convert_element_type.193, bf16[3072,1536]{1,0:T(8,128)(2,1)} %bitcast.120, f32[3072]{0:T(1024)S(1)} %mul.706), kind=kOutput, calls=%fused_computation.21 | convolution fusion | flops 4834983936 | bytes 14168064 | tf_op jit(solution)/shard_map/qn,pn->pq/dot_general | solution.py:201
  596.5 4.1 all-to-all-start.4
  602.8 2.8 copy.55
  605.6 4.6 convert_element_type.172
  610.2 9.4 %multiply_convert_fusion.1 = bf16[512,3072]{1,0:T(8,128)(2,1)} fusion(bf16[512,1536]{1,0:T(8,128)(2,1)} %convert_element_type.172, bf16[3072,1536]{1,0:T(8,128)(2,1)} %bitcast.121, f32[3072]{0:T(1024)S(1)} %mul.706), kind=kOutput, calls=%fused_computation.22 | convolution fusion | flops 4834983936 | bytes 14168064 | tf_op jit(solution)/shard_map/qn,pn->pq/dot_general | solution.py:201
  619.7 51.7 %all-to-all-done.4 = bf16[8,64,3072]{2,1,0:T(8,128)(2,1)S(1)} async-done(((bf16[8,64,3072]{2,1,0:T(8,128)(2,1)}), bf16[8,64,3072]{2,1,0:T(8,128)(2,1)S(1)}, u32[]{:S(2)}, u32[]{:S(2)}) %all-to-all-start.4) | async-done | bytes 3145760 | tf_op jit(solution)/shard_map/all_to_all | solution.py:205
  671.4 4.5 all-to-all-start.3
  675.8 3.4 copy.80
  679.2 66.8 %all-to-all-done.3 = bf16[8,64,3072]{2,1,0:T(8,128)(2,1)} async-done(((bf16[8,64,3072]{2,1,0:T(8,128)(2,1)}), bf16[8,64,3072]{2,1,0:T(8,128)(2,1)}, u32[]{:S(2)}, u32[]{:S(2)}) %all-to-all-start.3) | async-done | bytes 3145760 | tf_op jit(solution)/shard_map/all_to_all | solution.py:205
  746.0 5.2 copy.76
  751.3 15.0 %reshape.1482 = bf16[32,2,768,32]{3,2,1,0:T(8,128)(2,1)} reshape(bf16[64,8,3072]{2,1,0:T(8,128)(2,1)} %copy.76) | data formatting | bytes 6291456 | tf_op jit(solution)/shard_map/reshape | solution.py:208
  766.3 11.0 %reshape.1483 = bf16[32,2,768,32]{3,2,1,0:T(8,128)(2,1)} reshape(bf16[64,8,3072]{2,1,0:T(8,128)(2,1)S(1)} %copy-done) | data formatting | bytes 6291456 | tf_op jit(solution)/shard_map/reshape | solution.py:208
  777.2 42.9 %fusion.38 = bf16[32,2,32,512]{3,2,1,0:T(8,128)(2,1)S(1)} fusion(bf16[32,2,32,768]{2,3,1,0:T(8,128)(2,1)} %bitcast.115, bf16[512,32,768,1]{2,1,0,3:T(8,128)(2,1)} %bitcast.112), kind=kOutput, calls=%fused_computation.42 | convolution fusion | flops 1611661312 | bytes 30408704 | tf_op jit(solution)/shard_map/scij,lsj->scil/dot_general | solution.py:211
  820.1 44.3 %fusion.41 = bf16[32,2,32,512]{3,2,1,0:T(8,128)(2,1)} fusion(bf16[32,2,32,768]{2,3,1,0:T(8,128)(2,1)} %bitcast.114, bf16[512,32,768,1]{2,1,0,3:T(8,128)(2,1)} %bitcast.110), kind=kOutput, calls=%fused_computation.43 | convolution fusion | flops 1611661312 | bytes 30408704 | tf_op jit(solution)/shard_map/scij,lsj->scil/dot_general | solution.py:211
  864.5 4.0 pad_maximum_fusion
  (56 shorter events, 18.1 us)
Async XLA Ops:
  48.0 99.7 %all-to-all-start = ((bf16[64,2,2,128,128]{3,2,0,1,4:T(2,128)(2,1)}), bf16[64,2,2,128,128]{3,2,0,1,4:T(2,128)(2,1)}, u32[]{:S(2)}, u32[]{:S(2)}) async-start(bf16[64,2,2,128,128]{3,2,0,1,4:T(2,128)(2,1)} %copy.60), calls=%async_computation | async-start | bytes 16777216 | tf_op jit(solution)/shard_map/all_to_all | solution.py:159
  206.9 144.7 %all-to-all-start.2 = ((bf16[32,768,128]{2,0,1:T(8,128)(2,1)}), bf16[32,768,128]{2,0,1:T(8,128)(2,1)}, u32[]{:S(2)}, u32[]{:S(2)}) async-start(bf16[32,768,128]{2,0,1:T(8,128)(2,1)} %copy.70), calls=%async_computation.2 | async-start | bytes 12582912 | tf_op jit(solution)/shard_map/all_to_all | solution.py:172
  281.3 75.2 %copy-start.7 = (s32[512]{0:T(512)S(1)}, s32[512]{0:T(512)}, u32[]{:S(2)}) copy-start(s32[512]{0:T(512)} %param.7) | copy-start | bytes 6148
  351.6 142.2 %all-to-all-start.1 = ((bf16[32,768,128]{2,0,1:T(8,128)(2,1)}), bf16[32,768,128]{2,0,1:T(8,128)(2,1)}, u32[]{:S(2)}, u32[]{:S(2)}) async-start(bf16[32,768,128]{2,0,1:T(8,128)(2,1)} %copy.63), calls=%async_computation.1 | async-start | bytes 12582912 | tf_op jit(solution)/shard_map/all_to_all | solution.py:172
  528.2 11.1 %copy-start.2 = (bf16[256,96,1,2,32]{0,4,3,1,2:T(8,128)(2,1)S(1)}, bf16[256,96,1,2,32]{0,4,3,1,2:T(8,128)(2,1)}, u32[]{:S(2)}) copy-start(bf16[256,96,1,2,32]{0,4,3,1,2:T(8,128)(2,1)} %copy.105) | copy-start | bytes 9437188
  528.2 11.1 %copy-start.5 = (bf16[256,1,1536]{2,0,1:T(8,128)(2,1)S(1)}, bf16[256,1,1536]{2,0,1:T(8,128)(2,1)}, u32[]{:S(2)}) copy-start(bf16[256,1,1536]{2,0,1:T(8,128)(2,1)} %get-tuple-element.24) | copy-start | bytes 2359300
  528.2 11.1 %copy-start.6 = (bf16[256,1,1536]{2,0,1:T(8,128)(2,1)S(1)}, bf16[256,1,1536]{2,0,1:T(8,128)(2,1)}, u32[]{:S(2)}) copy-start(bf16[256,1,1536]{2,0,1:T(8,128)(2,1)} %get-tuple-element.25) | copy-start | bytes 2359300
  539.2 9.5 %copy-start.1 = (bf16[256,96,1,2,32]{0,4,3,1,2:T(8,128)(2,1)S(1)}, bf16[256,96,1,2,32]{0,4,3,1,2:T(8,128)(2,1)}, u32[]{:S(2)}) copy-start(bf16[256,96,1,2,32]{0,4,3,1,2:T(8,128)(2,1)} %copy.106) | copy-start | bytes 9437188
  539.3 9.4 %copy-start.3 = (bf16[256,1,1536]{2,0,1:T(8,128)(2,1)S(1)}, bf16[256,1,1536]{2,0,1:T(8,128)(2,1)}, u32[]{:S(2)}) copy-start(bf16[256,1,1536]{2,0,1:T(8,128)(2,1)} %get-tuple-element.29) | copy-start | bytes 2359300
  539.3 9.4 %copy-start.4 = (bf16[256,1,1536]{2,0,1:T(8,128)(2,1)S(1)}, bf16[256,1,1536]{2,0,1:T(8,128)(2,1)}, u32[]{:S(2)}) copy-start(bf16[256,1,1536]{2,0,1:T(8,128)(2,1)} %get-tuple-element.30) | copy-start | bytes 2359300
  596.5 74.8 %all-to-all-start.4 = ((bf16[8,64,3072]{2,1,0:T(8,128)(2,1)}), bf16[8,64,3072]{2,1,0:T(8,128)(2,1)S(1)}, u32[]{:S(2)}, u32[]{:S(2)}) async-start(bf16[8,64,3072]{2,1,0:T(8,128)(2,1)} %bitcast.118), calls=%async_computation.4 | async-start | bytes 6291456 | tf_op jit(solution)/shard_map/all_to_all | solution.py:205
  671.4 74.7 %all-to-all-start.3 = ((bf16[8,64,3072]{2,1,0:T(8,128)(2,1)}), bf16[8,64,3072]{2,1,0:T(8,128)(2,1)}, u32[]{:S(2)}, u32[]{:S(2)}) async-start(bf16[8,64,3072]{2,1,0:T(8,128)(2,1)} %bitcast.119), calls=%async_computation.3 | async-start | bytes 6291456 | tf_op jit(solution)/shard_map/all_to_all | solution.py:205
  751.3 15.0 %copy-start = (bf16[64,8,3072]{2,1,0:T(8,128)(2,1)S(1)}, bf16[64,8,3072]{2,1,0:T(8,128)(2,1)}, u32[]{:S(2)}) copy-start(bf16[64,8,3072]{2,1,0:T(8,128)(2,1)} %copy.80) | copy-start | bytes 9437188
